TPU v7x, 32 devices: a whole 2x2x4 slice. The times are simulated.
32 devices in a mesh: grp: 8 (over z, y), bfly: 4 (over x, core).
Axes of the slice: x: 2, y: 2, z: 4, core: 2. Of those that a mesh axis runs over, the one named last changes fastest.
Arguments:
- sources: bfloat16 [8, 4, 16, 256, 1024], P('grp', 'bfly'), may hold values from -6 to 6
- box_map: int32 [8, 4, 16], P('grp', 'bfly'), may hold values from 0 to 15, each once within a row
- compress: bfloat16 [8, 4, 16, 64, 256], P('grp', 'bfly'), may hold values from -0.375 to 0.375
- translate: bfloat16 [8, 4, 12, 16, 64, 128], P('grp', 'bfly'), may hold values from -0.5 to 0.5
- expand: bfloat16 [4, 16, 64, 256], P('bfly'), may hold values from -0.25 to 0.25
Outputs:
- field: bfloat16 [4, 16, 256, 1024], P('bfly', 'grp')
All inputs are finite; a program needn't handle non-finite values.
Results may differ from a plain program's by a relative error of at most 0.03.
Values may be sent and summed in bfloat16 or wider, within the bound.
A program may use at most 128 MiB of HBM per device.

v0:
```python
import jax
import jax.numpy as jnp
from jax import lax
from jax.sharding import PartitionSpec as P


def swapped(value, axis, apart):
    mask = 2**apart
    pairs = [(source, source ^ mask) for source in range(lax.axis_size(axis))]
    return lax.ppermute(value, axis, pairs)


def expand_exact(maps, summed):
    upper = summed.astype(jnp.bfloat16)
    lower = (summed - upper.astype(jnp.float32)).astype(jnp.bfloat16)
    first = jnp.einsum("jri,jrv->jiv", maps, upper, preferred_element_type=jnp.float32)
    return first + jnp.einsum("jri,jrv->jiv", maps, lower, preferred_element_type=jnp.float32)


def on_device(sources, box_map, compress, translate, expand):
    slot_order = box_map[0, 0]
    placed = jnp.take(sources[0, 0], slot_order, axis=0)
    coeffs = jnp.einsum(
        "jri,jiv->jrv", compress[0, 0], placed, preferred_element_type=jnp.float32
    ).astype(jnp.bfloat16)
    bfly_size = lax.axis_size("bfly")
    bit_count = bfly_size.bit_length() - 1
    levels = translate.shape[2]
    slots = translate.shape[3]
    rank = translate.shape[4]
    slot_bits = slots.bit_length() - 1
    for section_no in range(levels):
        matrices = translate[0, 0, section_no]
        own_part = jnp.einsum(
            "jrs,jsv->jrv", matrices[:, :, :rank], coeffs, preferred_element_type=jnp.float32
        )
        if section_no < bit_count:
            partner = swapped(coeffs, "bfly", section_no)
        else:
            stride = 1 << (section_no - bit_count) % slot_bits
            paired = coeffs.reshape((slots // (2 * stride), 2, stride) + coeffs.shape[1:])
            partner = paired[:, ::-1].reshape(coeffs.shape)
        updated = own_part + jnp.einsum(
            "jrs,jsv->jrv", matrices[:, :, rank:], partner, preferred_element_type=jnp.float32
        )
        if section_no < levels - 1:
            coeffs = updated.astype(jnp.bfloat16)
        else:
            coeffs = updated
    expand_rows = expand[0]
    gathered = lax.psum_scatter(
        coeffs.astype(jnp.bfloat16), "grp", scatter_dimension=0, tiled=True
    ).astype(jnp.float32)
    share_rows = gathered.shape[0]
    own_maps = lax.dynamic_slice_in_dim(
        expand_rows, lax.axis_index("grp") * share_rows, share_rows, 0
    )
    share = expand_exact(own_maps, gathered)
    return share.astype(jnp.bfloat16)[None]


def solution(mesh):
    return jax.shard_map(
        on_device,
        mesh=mesh,
        in_specs=(
            P("grp", "bfly", None, None, None),
            P("grp", "bfly", None),
            P("grp", "bfly", None, None, None),
            P("grp", "bfly", None, None, None, None),
            P("bfly", None, None, None),
        ),
        out_specs=P("bfly", "grp", None, None),
        check_vma=False,
    )
```

profile of v0, /device:TPU:0, one launch (start us, length us, event | category | flops | bytes accessed | tf_op | source)
XLA Modules:
  0.0 236.8 jit_solution(14294151172046835573)
XLA Ops:
  7.9 8.1 %gather_fusion = bf16[16,256,1024]{2,1,0:T(8,128)(2,1)} fusion(bf16[16,256,1024]{2,1,0:T(8,128)(2,1)} %bitcast.120, s32[1024]{0:T(1024)S(1)} %pad_clamp_fusion), kind=kCustom, calls=%fused_computation | custom fusion | bytes 16777280 | tf_op jit(solution)/shard_map/jit(_take)/gather | solution.py:22
  16.1 5.5 %fusion.4 = bf16[16,1024,64]{1,2,0:T(8,128)(2,1)S(1)} fusion(bf16[16,256,1024]{2,1,0:T(8,128)(2,1)} %gather_fusion, pred[16]{0:T(512)(128)(4,1)S(1)} %compare_and_fusion, bf16[1,1,16,64,256]{4,3,2,1,0:T(8,128)(2,1)S(1)} %copy-done), kind=kOutput, calls=%fused_computation.18 | convolution fusion | flops 542113792 | bytes 11010064 | tf_op jit(solution)/shard_map/jri,jiv->jrv/dot_general | solution.py:23
  26.6 2.9 %collective-permute-start.1 = (bf16[16,64,1024]{2,1,0:T(8,128)(2,1)S(1)}, bf16[16,64,1024]{2,1,0:T(8,128)(2,1)S(1)}, u32[]{:S(2)}, u32[]{:S(2)}) collective-permute-start(bf16[16,64,1024]{2,1,0:T(8,128)(2,1)S(1)} %bitcast.121), channel_id=1, source_target_pairs={{0,2},{1,3},{2,0},{3,1},{4,6},{5,7},{6,4},{7,5},{8,10},{9,11},{10,... | collective-permute-start | bytes 6291464 | tf_op jit(solution)/shard_map/ppermute | solution.py:10
  30.2 45.3 %collective-permute-done.1 = bf16[16,64,1024]{2,1,0:T(8,128)(2,1)S(1)} collective-permute-done((bf16[16,64,1024]{2,1,0:T(8,128)(2,1)S(1)}, bf16[16,64,1024]{2,1,0:T(8,128)(2,1)S(1)}, u32[]{:S(2)}, u32[]{:S(2)}) %collective-permute-start.1) | collective-permute-done | bytes 2097184 | tf_op jit(solution)/shard_map/ppermute | solution.py:10
  76.3 2.6 %fusion.26 = f32[16,1024,64]{1,2,0:T(8,128)} fusion(bf16[16,1024,64]{1,2,0:T(8,128)(2,1)S(1)} %add_convert_fusion.10, bf16[16,64,128]{2,1,0:T(8,128)(2,1)S(1)} %get-tuple-element.13), kind=kOutput, calls=%fused_computation.39 | convolution fusion | flops 134217728 | bytes 6553600 | tf_op jit(solution)/shard_map/jrs,jsv->jrv/dot_general | solution.py:34
  80.5 3.7 %add_convert_fusion.9 = bf16[16,1024,64]{1,2,0:T(8,128)(2,1)S(1)} fusion(f32[16,1024,64]{1,2,0:T(8,128)} %fusion.26, bf16[16,64,1024]{2,1,0:T(8,128)(2,1)} %bitcast.122, bf16[16,64,128]{2,1,0:T(8,128)(2,1)} %copy-done.7), kind=kOutput, calls=%fused_computation.13 | convolution fusion | flops 136314880 | bytes 8650752 | tf_op jit(solution)/shard_map/jrs,jsv->jrv/dot_general | solution.py:43
  84.2 2.6 %fusion.28 = f32[16,1024,64]{1,2,0:T(8,128)} fusion(bf16[16,1024,64]{1,2,0:T(8,128)(2,1)S(1)} %add_convert_fusion.9, bf16[16,64,128]{2,1,0:T(8,128)(2,1)S(1)} %copy-done.6), kind=kOutput, calls=%fused_computation.41 | convolution fusion | flops 134217728 | bytes 6553600 | tf_op jit(solution)/shard_map/jrs,jsv->jrv/dot_general | solution.py:34
  88.5 3.7 %add_convert_fusion.8 = bf16[16,1024,64]{1,2,0:T(8,128)(2,1)S(1)} fusion(f32[16,1024,64]{1,2,0:T(8,128)} %fusion.28, bf16[16,64,1024]{2,1,0:T(8,128)(2,1)} %bitcast.123, bf16[16,64,128]{2,1,0:T(8,128)(2,1)} %get-tuple-element.12), kind=kOutput, calls=%fused_computation.12 | convolution fusion | flops 136314880 | bytes 8650752 | tf_op jit(solution)/shard_map/jrs,jsv->jrv/dot_general | solution.py:43
  92.2 2.6 %fusion.30 = f32[16,1024,64]{1,2,0:T(8,128)} fusion(bf16[16,1024,64]{1,2,0:T(8,128)(2,1)S(1)} %add_convert_fusion.8, bf16[16,64,128]{2,1,0:T(8,128)(2,1)S(1)} %copy-done.5), kind=kOutput, calls=%fused_computation.43 | convolution fusion | flops 134217728 | bytes 6553600 | tf_op jit(solution)/shard_map/jrs,jsv->jrv/dot_general | solution.py:34
  96.4 3.7 %add_convert_fusion.7 = bf16[16,1024,64]{1,2,0:T(8,128)(2,1)S(1)} fusion(f32[16,1024,64]{1,2,0:T(8,128)} %fusion.30, bf16[16,64,1024]{2,1,0:T(8,128)(2,1)} %bitcast.124, bf16[16,64,128]{2,1,0:T(8,128)(2,1)} %get-tuple-element.11), kind=kOutput, calls=%fused_computation.11 | convolution fusion | flops 136314880 | bytes 8650752 | tf_op jit(solution)/shard_map/jrs,jsv->jrv/dot_general | solution.py:43
  100.1 2.6 %fusion.32 = f32[16,1024,64]{1,2,0:T(8,128)} fusion(bf16[16,1024,64]{1,2,0:T(8,128)(2,1)S(1)} %add_convert_fusion.7, bf16[16,64,128]{2,1,0:T(8,128)(2,1)S(1)} %copy-done.4), kind=kOutput, calls=%fused_computation.45 | convolution fusion | flops 134217728 | bytes 6553600 | tf_op jit(solution)/shard_map/jrs,jsv->jrv/dot_general | solution.py:34
  104.4 3.7 %add_convert_fusion.6 = bf16[16,1024,64]{1,2,0:T(8,128)(2,1)S(1)} fusion(f32[16,1024,64]{1,2,0:T(8,128)} %fusion.32, bf16[16,64,1024]{2,1,0:T(8,128)(2,1)} %bitcast.125, bf16[16,64,128]{2,1,0:T(8,128)(2,1)} %get-tuple-element.10), kind=kOutput, calls=%fused_computation.10 | convolution fusion | flops 136314880 | bytes 8650752 | tf_op jit(solution)/shard_map/jrs,jsv->jrv/dot_general | solution.py:43
  108.1 2.6 %fusion.34 = f32[16,1024,64]{1,2,0:T(8,128)} fusion(bf16[16,1024,64]{1,2,0:T(8,128)(2,1)S(1)} %add_convert_fusion.6, bf16[16,64,128]{2,1,0:T(8,128)(2,1)S(1)} %copy-done.3), kind=kOutput, calls=%fused_computation.47 | convolution fusion | flops 134217728 | bytes 6553600 | tf_op jit(solution)/shard_map/jrs,jsv->jrv/dot_general | solution.py:34
  112.3 3.9 %add_convert_fusion.5 = bf16[16,1024,64]{1,2,0:T(8,128)(2,1)S(1)} fusion(f32[16,1024,64]{1,2,0:T(8,128)} %fusion.34, bf16[16,64,1024]{2,1,0:T(8,128)(2,1)} %bitcast.126, bf16[16,64,128]{2,1,0:T(8,128)(2,1)} %get-tuple-element.9), kind=kOutput, calls=%fused_computation.9 | convolution fusion | flops 136314880 | bytes 8650752 | tf_op jit(solution)/shard_map/jrs,jsv->jrv/dot_general | solution.py:43
  116.2 2.6 %fusion.36 = f32[16,1024,64]{1,2,0:T(8,128)} fusion(bf16[16,1024,64]{1,2,0:T(8,128)(2,1)S(1)} %add_convert_fusion.5, bf16[16,64,128]{2,1,0:T(8,128)(2,1)S(1)} %get-tuple-element.8), kind=kOutput, calls=%fused_computation.49 | convolution fusion | flops 134217728 | bytes 6553600 | tf_op jit(solution)/shard_map/jrs,jsv->jrv/dot_general | solution.py:34
  120.4 3.6 %add_convert_fusion.4 = bf16[16,1024,64]{1,2,0:T(8,128)(2,1)S(1)} fusion(f32[16,1024,64]{1,2,0:T(8,128)} %fusion.36, bf16[16,64,1024]{2,1,0:T(8,128)(2,1)} %bitcast.127, bf16[16,64,128]{2,1,0:T(8,128)(2,1)S(1)} %get-tuple-element.8), kind=kOutput, calls=%fused_computation.8 | convolution fusion | flops 136314880 | bytes 8650752 | tf_op jit(solution)/shard_map/jrs,jsv->jrv/dot_general | solution.py:43
  124.0 2.6 %fusion.38 = f32[16,1024,64]{1,2,0:T(8,128)} fusion(bf16[16,1024,64]{1,2,0:T(8,128)(2,1)S(1)} %add_convert_fusion.4, bf16[16,64,128]{2,1,0:T(8,128)(2,1)S(1)} %get-tuple-element.7), kind=kOutput, calls=%fused_computation.51 | convolution fusion | flops 134217728 | bytes 6553600 | tf_op jit(solution)/shard_map/jrs,jsv->jrv/dot_general | solution.py:34
  128.2 3.6 %add_convert_fusion.3 = bf16[16,1024,64]{1,2,0:T(8,128)(2,1)S(1)} fusion(f32[16,1024,64]{1,2,0:T(8,128)} %fusion.38, bf16[16,64,1024]{2,1,0:T(8,128)(2,1)} %bitcast.128, bf16[16,64,128]{2,1,0:T(8,128)(2,1)S(1)} %get-tuple-element.7), kind=kOutput, calls=%fused_computation.7 | convolution fusion | flops 136314880 | bytes 8650752 | tf_op jit(solution)/shard_map/jrs,jsv->jrv/dot_general | solution.py:43
  131.8 2.6 %fusion.40 = f32[16,1024,64]{1,2,0:T(8,128)} fusion(bf16[16,1024,64]{1,2,0:T(8,128)(2,1)S(1)} %add_convert_fusion.3, bf16[16,64,128]{2,1,0:T(8,128)(2,1)S(1)} %get-tuple-element.6), kind=kOutput, calls=%fused_computation.53 | convolution fusion | flops 134217728 | bytes 6553600 | tf_op jit(solution)/shard_map/jrs,jsv->jrv/dot_general | solution.py:34
  136.0 3.6 %add_convert_fusion.2 = bf16[16,1024,64]{1,2,0:T(8,128)(2,1)S(1)} fusion(f32[16,1024,64]{1,2,0:T(8,128)} %fusion.40, bf16[16,64,1024]{2,1,0:T(8,128)(2,1)} %bitcast.129, bf16[16,64,128]{2,1,0:T(8,128)(2,1)S(1)} %get-tuple-element.6), kind=kOutput, calls=%fused_computation.6 | convolution fusion | flops 136314880 | bytes 8650752 | tf_op jit(solution)/shard_map/jrs,jsv->jrv/dot_general | solution.py:43
  139.6 2.6 %fusion.42 = f32[16,1024,64]{1,2,0:T(8,128)} fusion(bf16[16,1024,64]{1,2,0:T(8,128)(2,1)S(1)} %add_convert_fusion.2, bf16[16,64,128]{2,1,0:T(8,128)(2,1)S(1)} %get-tuple-element.16), kind=kOutput, calls=%fused_computation.55 | convolution fusion | flops 134217728 | bytes 6553600 | tf_op jit(solution)/shard_map/jrs,jsv->jrv/dot_general | solution.py:34
  143.8 3.6 %add_convert_fusion.1 = bf16[16,1024,64]{1,2,0:T(8,128)(2,1)S(1)} fusion(f32[16,1024,64]{1,2,0:T(8,128)} %fusion.42, bf16[16,64,1024]{2,1,0:T(8,128)(2,1)} %bitcast.130, bf16[16,64,128]{2,1,0:T(8,128)(2,1)S(1)} %get-tuple-element.16), kind=kOutput, calls=%fused_computation.5 | convolution fusion | flops 136314880 | bytes 8650752 | tf_op jit(solution)/shard_map/jrs,jsv->jrv/dot_general | solution.py:43
  151.7 4.9 %fusion.7 = bf16[16,64,1024]{2,1,0:T(8,128)(2,1)} fusion(f32[16,1024,64]{1,2,0:T(8,128)} %fusion.44, bf16[16,64,1024]{2,1,0:T(8,128)(2,1)} %bitcast.131, bf16[16,64,128]{2,1,0:T(8,128)(2,1)S(1)} %get-tuple-element.5), kind=kOutput, calls=%fused_computation.19 | convolution fusion | flops 136314880 | bytes 8650752 | tf_op jit(solution)/shard_map/jrs,jsv->jrv/dot_general | solution.py:43
  156.6 69.5 %reduce-scatter.2.cloned.1.call-done = bf16[2,64,1024]{2,1,0:T(8,128)(2,1)} async-done(((bf16[16,64,1024]{2,1,0:T(8,128)(2,1)}), bf16[2,64,1024]{2,1,0:T(8,128)(2,1)}) %reduce-scatter.2.cloned.1.call-update) | async-done | bytes 262160 | tf_op jit(solution)/shard_map/reduce_scatter | solution.py:51
  (43 shorter events, 30.3 us)
Async XLA Ops:
  6.5 9.5 %copy-start = (bf16[1,1,16,64,256]{4,3,2,1,0:T(8,128)(2,1)S(1)}, bf16[1,1,16,64,256]{4,3,2,1,0:T(8,128)(2,1)}, u32[]{:S(2)}) copy-start(bf16[1,1,16,64,256]{4,3,2,1,0:T(8,128)(2,1)} %param.7) | copy-start | bytes 1572868
  6.5 219.6 %reduce-scatter.2.cloned.1.call-start = ((), (), s32[]{:S(2)}) async-start(), calls=%async_computation.1 | async-start | bytes 2359296 | tf_op jit(solution)/shard_map/reduce_scatter | solution.py:51
  16.1 6.0 %copy-start.2 = (bf16[1,1,12,16,64,128]{5,4,3,2,1,0:T(8,128)(2,1)S(1)}, bf16[1,1,12,16,64,128]{5,4,3,2,1,0:T(8,128)(2,1)}, u32[]{:S(2)}) copy-start(bf16[1,1,12,16,64,128]{5,4,3,2,1,0:T(8,128)(2,1)} %param.8) | copy-start | bytes 9437188
  21.6 4.3 %collective-permute-start = (bf16[16,64,1024]{2,1,0:T(8,128)(2,1)S(1)}, bf16[16,64,1024]{2,1,0:T(8,128)(2,1)S(1)}, u32[]{:S(2)}, u32[]{:S(2)}) collective-permute-start(bf16[16,64,1024]{2,1,0:T(8,128)(2,1)S(1)} %bitcast.132), channel_id=1, source_target_pairs={{0,1},{1,0},{2,3},{3,2},{4,5},{5,4},{6,7},{7,6},{8,9},{9,8},{10,11... | collective-permute-start | bytes 6291464 | tf_op jit(solution)/shard_map/ppermute | solution.py:10
  23.6 52.6 %copy-start.7 = (bf16[16,64,128]{2,1,0:T(8,128)(2,1)}, bf16[16,64,128]{2,1,0:T(8,128)(2,1)S(1)}, u32[]{:S(2)}) copy-start(bf16[16,64,128]{2,1,0:T(8,128)(2,1)S(1)} %get-tuple-element.13) | copy-start | bytes 786436
  26.6 48.9 %collective-permute-start.1 = (bf16[16,64,1024]{2,1,0:T(8,128)(2,1)S(1)}, bf16[16,64,1024]{2,1,0:T(8,128)(2,1)S(1)}, u32[]{:S(2)}, u32[]{:S(2)}) collective-permute-start(bf16[16,64,1024]{2,1,0:T(8,128)(2,1)S(1)} %bitcast.121), channel_id=1, source_target_pairs={{0,2},{1,3},{2,0},{3,1},{4,6},{5,7},{6,4},{7,5},{8,10},{9,11},{10,... | collective-permute-start | bytes 6291464 | tf_op jit(solution)/shard_map/ppermute | solution.py:10
  80.5 3.7 %copy-start.6 = (bf16[16,64,128]{2,1,0:T(8,128)(2,1)S(1)}, bf16[16,64,128]{2,1,0:T(8,128)(2,1)}, u32[]{:S(2)}) copy-start(bf16[16,64,128]{2,1,0:T(8,128)(2,1)} %get-tuple-element.12) | copy-start | bytes 786436
  88.5 3.7 %copy-start.5 = (bf16[16,64,128]{2,1,0:T(8,128)(2,1)S(1)}, bf16[16,64,128]{2,1,0:T(8,128)(2,1)}, u32[]{:S(2)}) copy-start(bf16[16,64,128]{2,1,0:T(8,128)(2,1)} %get-tuple-element.11) | copy-start | bytes 786436
  96.4 3.7 %copy-start.4 = (bf16[16,64,128]{2,1,0:T(8,128)(2,1)S(1)}, bf16[16,64,128]{2,1,0:T(8,128)(2,1)}, u32[]{:S(2)}) copy-start(bf16[16,64,128]{2,1,0:T(8,128)(2,1)} %get-tuple-element.10) | copy-start | bytes 786436
  104.4 3.7 %copy-start.3 = (bf16[16,64,128]{2,1,0:T(8,128)(2,1)S(1)}, bf16[16,64,128]{2,1,0:T(8,128)(2,1)}, u32[]{:S(2)}) copy-start(bf16[16,64,128]{2,1,0:T(8,128)(2,1)} %get-tuple-element.9) | copy-start | bytes 786436
  226.1 1.5 copy-start.8
  226.1 3.8 %copy-start.1 = (bf16[1,1,16,64,256]{4,3,2,1,0:T(8,128)(2,1)S(1)}, bf16[1,1,16,64,256]{4,3,2,1,0:T(8,128)(2,1)}, u32[]{:S(2)}) copy-start(bf16[1,1,16,64,256]{4,3,2,1,0:T(8,128)(2,1)} %param.7) | copy-start | bytes 1572868
Sparse Core Ops, SparseCore 0:
  156.7 69.3 reduce-scatter.1
where the time goes:
time: 237 us
  waiting for transfers between devices  116 us (49%)
  matrix products  76.5 us (32%)
  local copies, waits for them, and re-layouts  25.6 us (11%)
  between operations  13.5 us (6%)
  starting transfers between devices  3.43 us (1%)
    reduce_scatter x1, waiting for transfers between devices, on_device(): lax.psum_scatter(coeffs.astype(jnp.bfloat16), 'grp', scatter_dimension=0,...  69.5 us
    ppermute x2, waiting for transfers between devices, swapped(): return lax.ppermute(value, axis, pairs)  46.8 us
    dot_general x12, matrix products, on_device(): jnp.einsum('jrs,jsv->jrv', matrices[:, :, rank:], partner, preferred_elem...  39.4 us
    dot_general x12, matrix products, on_device(): jnp.einsum('jrs,jsv->jrv', matrices[:, :, :rank], coeffs, preferred_eleme...  27.8 us
    rev x10, local copies, waits for them, and re-layouts, on_device(): partner = paired[:, ::-1].reshape(coeffs.shape)  15.9 us
    gather x1, local copies, waits for them, and re-layouts, on_device(): placed = jnp.take(sources[0, 0], slot_order, axis=0)  8.14 us
    dot_general x1, matrix products, on_device(): jnp.einsum('jri,jiv->jrv', compress[0, 0], placed, preferred_element_type...  5.5 us
  transfers between devices with their start and end apart: 3, of which 3 were waited for; matrix products, arithmetic and copies ran while one was open for 1% of the time, Pallas kernels for 0%

commit v1 on v0

v1 whole, which is shorter than its diff:
```python
import functools

import jax
import jax.numpy as jnp
from jax import lax
from jax.experimental import pallas as pl
from jax.experimental.pallas import tpu as pltpu
from jax.sharding import PartitionSpec as P

MESH = pl.DeviceIdType.MESH
F32 = jnp.float32
BF16 = jnp.bfloat16
CHUNKS = 4


def dot(a, b):
    return jnp.dot(a, b, preferred_element_type=F32)


def swap_halves(m):
    half = m.shape[1] // 2
    return jnp.concatenate([m[:, half:], m[:, :half]], axis=1)


class Plan:
    def __init__(self, n_grp, n_bfly, sources, compress, translate, expand):
        self.n_bfly = n_bfly
        self.bits = n_bfly.bit_length() - 1
        self.slots, self.rank, self.box = compress.shape[2:]
        self.levels = translate.shape[2]
        self.nv = sources.shape[-1]
        self.chunks = CHUNKS
        self.width = self.nv // self.chunks
        self.outer = min(4, n_grp)
        self.inner = n_grp // self.outer
        self.share = self.slots // n_grp
        self.pairs = (self.levels - self.bits) // 2
        assert self.slots == 16 and self.bits >= 1
        assert (self.levels - self.bits) % 2 == 0

    def strided(self, pair):
        return (2 * pair) % 4 == 2

    def member(self, pair, quad, place):
        return 4 * place + quad if self.strided(pair) else 4 * quad + place


def kernel(plan, map_ref, src_hbm, comp_hbm, trans_hbm, exp_hbm, out_hbm, *scratch):
    C, B, S, R = plan.chunks, plan.bits, plan.slots, plan.rank
    W, inner, outer, share = plan.width, plan.inner, plan.outer, plan.share
    scratch = list(scratch)
    src = [scratch.pop(0) for _ in range(C)]
    cats = [scratch.pop(0) for _ in range(B)]
    (comp, trans, expand, merged, wide, ping, pong, part, got_in, mid, got_out, done,
     src_sem, par_sem, out_sem, bsend, brecv, isend, irecv, osend, orecv) = scratch
    grp = lax.axis_index("grp")
    bfly = lax.axis_index("bfly")
    my_out, my_in = grp // inner, grp % inner

    def partner(level):
        bit = (bfly // (1 << level)) % 2
        return bfly + (1 << level) * (1 - 2 * bit)

    src_copies = [
        pltpu.make_async_copy(src_hbm.at[0, 0, :, :, pl.ds(c * W, W)], src[c], src_sem.at[c])
        for c in range(C)
    ]
    comp_copy = pltpu.make_async_copy(comp_hbm.at[0, 0], comp, par_sem.at[0])
    near_copy = pltpu.make_async_copy(trans_hbm.at[0, 0, pl.ds(0, B)], trans.at[pl.ds(0, B)], par_sem.at[1])
    rest_copy = pltpu.make_async_copy(
        trans_hbm.at[0, 0, pl.ds(B, plan.levels - B)], trans.at[pl.ds(B, plan.levels - B)], par_sem.at[2]
    )
    exp_copy = pltpu.make_async_copy(exp_hbm.at[0, pl.ds(grp * share, share)], expand, par_sem.at[3])
    comp_copy.start()
    src_copies[0].start()
    near_copy.start()
    for c in range(1, C):
        src_copies[c].start()
    rest_copy.start()
    exp_copy.start()

    peers = [(grp, partner(level)) for level in range(B)]
    in_peers = [(my_out * inner + (my_in + k) % inner, bfly) for k in range(1, inner)]
    out_peers = [(((my_out + k) % outer) * inner + my_in, bfly) for k in range(1, outer)]
    barrier = pltpu.get_barrier_semaphore()
    everyone = peers + in_peers + out_peers
    for peer in everyone:
        pl.semaphore_signal(barrier, inc=1, device_id=peer, device_id_type=MESH)
    pl.semaphore_wait(barrier, len(everyone))

    sends = []
    arrivals = {}

    def remote(key, source, target, send, recv, peer):
        copy = pltpu.make_async_remote_copy(
            src_ref=source, dst_ref=target, send_sem=send, recv_sem=recv,
            device_id=peer, device_id_type=MESH,
        )
        copy.start()
        sends.append(copy)
        arrivals[key] = copy

    def exchange(level, c):
        remote(
            ("b", level, c),
            cats[level].at[c, :, pl.ds(0, R)],
            cats[level].at[c, :, pl.ds(R, R)],
            bsend.at[level, c],
            brecv.at[level, c],
            peers[level],
        )

    def compress_stage(c):
        src_copies[c].wait()
        if c == 0:
            comp_copy.wait()
        for j in range(S):
            cats[0][c, j, 0:R, :] = dot(comp[j], src[c][map_ref[0, 0, j]]).astype(BF16)
        exchange(0, c)

    def far_stage(level, c):
        if c == 0 and level == 0:
            near_copy.wait()
        arrivals[("b", level, c)].wait_recv()
        for j in range(S):
            cats[level + 1][c, j, 0:R, :] = dot(trans[level, j], cats[level][c, j]).astype(BF16)
        exchange(level + 1, c)

    def merge_stage():
        rest_copy.wait()
        exp_copy.wait()
        for pair in range(plan.pairs):
            low = B + 2 * pair
            for quad in range(4):
                for place in range(4):
                    own = trans[low, plan.member(pair, quad, place)]
                    far = trans[low, plan.member(pair, quad, place ^ 2)]
                    if place & 1:
                        own, far = swap_halves(own), swap_halves(far)
                    zero = jnp.zeros_like(own)
                    if place & 2:
                        top, bottom = [zero, own], [far, zero]
                    else:
                        top, bottom = [own, zero], [zero, far]
                    block = jnp.concatenate(
                        [jnp.concatenate(top, axis=1), jnp.concatenate(bottom, axis=1)], axis=0
                    )
                    row = dot(trans[low + 1, plan.member(pair, quad, place)], block)
                    merged[pair, quad, place * R:(place + 1) * R, :] = row.astype(BF16)
        for s in range(share):
            wide[s] = expand[s].astype(F32).T.astype(BF16)

    def levels_stage(c):
        level = B - 1
        if level == 0 and c == 0:
            near_copy.wait()
        arrivals[("b", level, c)].wait_recv()
        for j in range(S):
            ping[j // 4, j % 4] = dot(trans[level, j], cats[level][c, j]).astype(BF16)
        now, later = ping, pong
        for pair in range(plan.pairs):
            for quad in range(4):
                picked = now[:, quad] if plan.strided(pair) else now[quad]
                value = dot(merged[pair, quad], picked.reshape(4 * R, W)).astype(BF16)
                value = value.reshape(4, R, W)
                if pair < plan.pairs - 1:
                    if plan.strided(pair):
                        later[:, quad] = value
                    else:
                        later[quad] = value
                else:
                    for place in range(4):
                        j = plan.member(pair, quad, place)
                        s, row = j // share, (j % share) * R
                        part[c, s % inner, s // inner, row:row + R, :] = value[place]
            now, later = later, now
        for k in range(1, inner):
            remote(
                ("i", k, c),
                part.at[c, (my_in + k) % inner],
                got_in.at[c, k - 1],
                isend.at[c, k - 1],
                irecv.at[c, k - 1],
                in_peers[k - 1],
            )

    def inner_stage(c):
        for k in range(1, inner):
            arrivals[("i", k, c)].wait_recv()
        total = part[c, my_in].astype(F32)
        for k in range(1, inner):
            total = total + got_in[c, k - 1].astype(F32)
        mid[c] = total.astype(BF16)
        for k in range(1, outer):
            remote(
                ("o", k, c),
                mid.at[c, (my_out + k) % outer],
                got_out.at[c, k - 1],
                osend.at[c, k - 1],
                orecv.at[c, k - 1],
                out_peers[k - 1],
            )

    out_copies = []

    def outer_stage(c):
        for k in range(1, outer):
            arrivals[("o", k, c)].wait_recv()
        total = mid[c, my_out].astype(F32)
        for k in range(1, outer):
            total = total + got_out[c, k - 1].astype(F32)
        upper = total.astype(BF16)
        lower = (total - upper.astype(F32)).astype(BF16)
        for s in range(share):
            rows = slice(s * R, (s + 1) * R)
            done[c, s] = (dot(wide[s], upper[rows]) + dot(wide[s], lower[rows])).astype(BF16)
        copy = pltpu.make_async_copy(done.at[c], out_hbm.at[0, :, :, pl.ds(c * W, W)], out_sem.at[c])
        copy.start()
        out_copies.append(copy)

    for t in range(C + B - 1):
        for level in reversed(range(B - 1)):
            if 0 <= t - 1 - level < C:
                far_stage(level, t - 1 - level)
        if t < C:
            compress_stage(t)
    merge_stage()
    for t in range(C + 2):
        if 0 <= t - 1 < C:
            inner_stage(t - 1)
        if 0 <= t - 2 < C:
            outer_stage(t - 2)
        if t < C:
            levels_stage(t)
    for copy in sends:
        copy.wait_send()
    for copy in out_copies:
        copy.wait()


def on_device(n_grp, n_bfly, sources, box_map, compress, translate, expand):
    plan = Plan(n_grp, n_bfly, sources, compress, translate, expand)
    C, B, S, R, W = plan.chunks, plan.bits, plan.slots, plan.rank, plan.width
    inner, outer, share = plan.inner, plan.outer, plan.share
    vm = pltpu.VMEM
    sem = pltpu.SemaphoreType.DMA
    any_space = pl.BlockSpec(memory_space=pl.ANY)
    return pl.pallas_call(
        functools.partial(kernel, plan),
        out_shape=jax.ShapeDtypeStruct((1, share, plan.box, plan.nv), BF16),
        in_specs=[pl.BlockSpec(memory_space=pltpu.SMEM)] + [any_space] * 4,
        out_specs=any_space,
        scratch_shapes=[vm((S, plan.box, W), BF16) for _ in range(C)]
        + [vm((C, S, 2 * R, W), BF16) for _ in range(B)]
        + [
            vm((S, R, plan.box), BF16),
            vm((plan.levels, S, R, 2 * R), BF16),
            vm((share, R, plan.box), BF16),
            vm((plan.pairs, 4, 4 * R, 4 * R), BF16),
            vm((share, plan.box, R), BF16),
            vm((4, 4, R, W), BF16),
            vm((4, 4, R, W), BF16),
            vm((C, inner, outer, share * R, W), BF16),
            vm((C, max(inner - 1, 1), outer, share * R, W), BF16),
            vm((C, outer, share * R, W), BF16),
            vm((C, max(outer - 1, 1), share * R, W), BF16),
            vm((C, share, plan.box, W), BF16),
            sem((C,)),
            sem((4,)),
            sem((C,)),
            sem((B, C)),
            sem((B, C)),
            sem((C, max(inner - 1, 1))),
            sem((C, max(inner - 1, 1))),
            sem((C, max(outer - 1, 1))),
            sem((C, max(outer - 1, 1))),
        ],
        compiler_params=pltpu.CompilerParams(
            collective_id=0, has_side_effects=True, vmem_limit_bytes=56 * 1024 * 1024
        ),
    )(box_map, sources, compress, translate, expand)


def solution(mesh):
    return jax.shard_map(
        functools.partial(on_device, mesh.shape["grp"], mesh.shape["bfly"]),
        mesh=mesh,
        in_specs=(
            P("grp", "bfly", None, None, None),
            P("grp", "bfly", None),
            P("grp", "bfly", None, None, None),
            P("grp", "bfly", None, None, None, None),
            P("bfly", None, None, None),
        ),
        out_specs=P("bfly", "grp", None, None),
        check_vma=False,
    )
```

time: 237 us -> 75.4 us (0.32)
  waiting for transfers between devices: 116 us -> 0 us
  matrix products: 76.5 us -> 0 us
  Pallas kernels: 0 us -> 72.9 us
  local copies, waits for them, and re-layouts: 25.6 us -> 2.26 us
  between operations: 13.5 us -> 0.01 us
  starting transfers between devices: 3.43 us -> 0 us
    dot_general x27 -> x0, matrix products: 76.5 us -> none  [the longest x12 39.4 us: on_device(): jnp.einsum('jrs,jsv->jrv', matrices[:, :, rank:], partner, preferred_elem...]
    pallas_call x0 -> x1, Pallas kernels: none -> 72.9 us  [on_device(): pl.pallas_call(functools.partial(kernel, plan), out_shape=jax.ShapeDtypeS...]
    reduce_scatter x1 -> x0, waiting for transfers between devices: 69.5 us -> none  [on_device(): lax.psum_scatter(coeffs.astype(jnp.bfloat16), 'grp', scatter_dimension=0,...]
    ppermute x2 -> x0, waiting for transfers between devices: 46.8 us -> none  [swapped(): return lax.ppermute(value, axis, pairs)]
    rev x10 -> x0, local copies, waits for them, and re-layouts: 15.9 us -> none  [on_device(): partner = paired[:, ::-1].reshape(coeffs.shape)]
    gather x1 -> x0, local copies, waits for them, and re-layouts: 8.14 us -> none  [on_device(): placed = jnp.take(sources[0, 0], slot_order, axis=0)]
    ppermute x2 -> x0, starting transfers between devices: 3.43 us -> none  [swapped(): return lax.ppermute(value, axis, pairs)]
  transfers between devices with their start and end apart: 3 -> 0, of which waited for: 3 -> 0; matrix products, arithmetic and copies ran while one was open for 1% -> 0% of each run, Pallas kernels for 0% -> 0%
where the time goes in v1:
time: 75.4 us; the launch traced here: 75.2 us
  Pallas kernels  72.9 us (97%)
  local copies, waits for them, and re-layouts  2.26 us (3%)
    pallas_call x1, Pallas kernels, on_device(): pl.pallas_call(functools.partial(kernel, plan), out_shape=jax.ShapeDtypeS...  72.9 us
    unnamed x1, local copies, waits for them, and re-layouts  2.26 us

profile of v1, /device:TPU:0, one launch (start us, length us, event | category | flops | bytes accessed | tf_op | source)
XLA Modules:
  0.0 75.2 jit_solution(16194720754715000311)
XLA Ops:
  0.0 72.9 %shard_map.55 = bf16[1,2,256,1024]{3,2,1,0:T(8,128)(2,1)} custom-call(s32[1,1,16]{2,1,0:T(1,128)} %map_ref.1, bf16[1,1,16,256,1024]{4,3,2,1,0:T(8,128)(2,1)} %src_hbm.1, bf16[1,1,16,64,256]{4,3,2,1,0:T(8,128)(2,1)} %comp_hbm.1, bf16[1,1,12,16,64,128]{5,4,3,2,1,0:T(8,128)(2,1)} %trans_hbm.1, bf16[1,16,64,256]{3,2,1,0:T(8,128)(2,1)} %exp_hbm.1), custom_call_target="tpu_custom_call" | custom-call | tf_op jit(solution)/shard_map/pallas_call | solution.py:248
  72.9 2.3 %copy.7 = bf16[1,2,256,1024]{3,2,1,0:T(8,128)(2,1)} copy(bf16[1,2,256,1024]{3,2,1,0:T(8,128)(2,1)} %shard_map.55) | data formatting | bytes 2097152

commit v2 on v1

--- a/solution.py
+++ b/solution.py
@@ -10,7 +10,7 @@
 MESH = pl.DeviceIdType.MESH
 F32 = jnp.float32
 BF16 = jnp.bfloat16
-CHUNKS = 4
+CHUNKS = 8
 
 
 def dot(a, b):
@@ -79,6 +79,7 @@
     rest_copy.start()
     exp_copy.start()
 
+    block_order = sorted(range(1, outer), key=lambda z: abs(2 * z - outer)) + [0]
     peers = [(grp, partner(level)) for level in range(B)]
     in_peers = [(my_out * inner + (my_in + k) % inner, bfly) for k in range(1, inner)]
     out_peers = [(((my_out + k) % outer) * inner + my_in, bfly) for k in range(1, outer)]
@@ -174,32 +175,36 @@
                         s, row = j // share, (j % share) * R
                         part[c, s % inner, s // inner, row:row + R, :] = value[place]
             now, later = later, now
-        for k in range(1, inner):
-            remote(
-                ("i", k, c),
-                part.at[c, (my_in + k) % inner],
-                got_in.at[c, k - 1],
-                isend.at[c, k - 1],
-                irecv.at[c, k - 1],
-                in_peers[k - 1],
-            )
+        for z in block_order:
+            block = (my_out + z) % outer
+            for k in range(1, inner):
+                remote(
+                    ("i", k, z, c),
+                    part.at[c, (my_in + k) % inner, block],
+                    got_in.at[c, k - 1, block],
+                    isend.at[c, k - 1, z],
+                    irecv.at[c, k - 1, z],
+                    in_peers[k - 1],
+                )
 
     def inner_stage(c):
-        for k in range(1, inner):
-            arrivals[("i", k, c)].wait_recv()
-        total = part[c, my_in].astype(F32)
-        for k in range(1, inner):
-            total = total + got_in[c, k - 1].astype(F32)
-        mid[c] = total.astype(BF16)
-        for k in range(1, outer):
-            remote(
-                ("o", k, c),
-                mid.at[c, (my_out + k) % outer],
-                got_out.at[c, k - 1],
-                osend.at[c, k - 1],
-                orecv.at[c, k - 1],
-                out_peers[k - 1],
-            )
+        for z in block_order:
+            block = (my_out + z) % outer
+            for k in range(1, inner):
+                arrivals[("i", k, z, c)].wait_recv()
+            total = part[c, my_in, block].astype(F32)
+            for k in range(1, inner):
+                total = total + got_in[c, k - 1, block].astype(F32)
+            mid[c, block] = total.astype(BF16)
+            if z > 0:
+                remote(
+                    ("o", z, c),
+                    mid.at[c, block],
+                    got_out.at[c, z - 1],
+                    osend.at[c, z - 1],
+                    orecv.at[c, z - 1],
+                    out_peers[z - 1],
+                )
 
     out_copies = []
 
@@ -226,12 +231,12 @@
             compress_stage(t)
     merge_stage()
     for t in range(C + 2):
+        if t < C:
+            levels_stage(t)
         if 0 <= t - 1 < C:
             inner_stage(t - 1)
         if 0 <= t - 2 < C:
             outer_stage(t - 2)
-        if t < C:
-            levels_stage(t)
     for copy in sends:
         copy.wait_send()
     for copy in out_copies:
@@ -270,8 +275,8 @@
             sem((C,)),
             sem((B, C)),
             sem((B, C)),
-            sem((C, max(inner - 1, 1))),
-            sem((C, max(inner - 1, 1))),
+            sem((C, max(inner - 1, 1), outer)),
+            sem((C, max(inner - 1, 1), outer)),
             sem((C, max(outer - 1, 1))),
             sem((C, max(outer - 1, 1))),
         ],

time: 75.4 us -> 70.1 us (0.930)
  Pallas kernels: 72.9 us -> 67.7 us
    pallas_call x1, Pallas kernels: 72.9 us -> 67.7 us  [on_device(): pl.pallas_call(functools.partial(kernel, plan), out_shape=jax.ShapeDtypeS...]
where the time goes in v2:
time: 70.1 us; the launch traced here: 70 us
  Pallas kernels  67.7 us (97%)
  local copies, waits for them, and re-layouts  2.26 us (3%)
    pallas_call x1, Pallas kernels, on_device(): pl.pallas_call(functools.partial(kernel, plan), out_shape=jax.ShapeDtypeS...  67.7 us
    unnamed x1, local copies, waits for them, and re-layouts  2.26 us

profile of v2, /device:TPU:0, one launch (start us, length us, event | category | flops | bytes accessed | tf_op | source)
XLA Modules:
  0.0 70.0 jit_solution(14183418938131589498)
XLA Ops:
  0.0 67.7 %shard_map.55 = bf16[1,2,256,1024]{3,2,1,0:T(8,128)(2,1)} custom-call(s32[1,1,16]{2,1,0:T(1,128)} %map_ref.1, bf16[1,1,16,256,1024]{4,3,2,1,0:T(8,128)(2,1)} %src_hbm.1, bf16[1,1,16,64,256]{4,3,2,1,0:T(8,128)(2,1)} %comp_hbm.1, bf16[1,1,12,16,64,128]{5,4,3,2,1,0:T(8,128)(2,1)} %trans_hbm.1, bf16[1,16,64,256]{3,2,1,0:T(8,128)(2,1)} %exp_hbm.1), custom_call_target="tpu_custom_call" | custom-call | tf_op jit(solution)/shard_map/pallas_call | solution.py:253
  67.7 2.3 %copy.7 = bf16[1,2,256,1024]{3,2,1,0:T(8,128)(2,1)} copy(bf16[1,2,256,1024]{3,2,1,0:T(8,128)(2,1)} %shard_map.55) | data formatting | bytes 2097152
